TPU v7x, 32 devices: a whole 2x2x4 slice. The times are simulated.
32 devices in a mesh: pole: 2 (over x), row: 4 (over y, core), col: 4 (over z).
Axes of the slice: x: 2, y: 2, z: 4, core: 2. Of those that a mesh axis runs over, the one named last changes fastest.
Arguments:
- known_inverse: float32 [4096, 2048], P(('pole', 'row'), 'col'), parts along dimension 0, may hold values from -1 to 2.5, as said below
- lower_first: float32 [4096, 512], P(('pole', 'row'), 'col'), parts along dimension 0, may hold values from -0.12 to 0.12
- lower_second: float32 [4096, 512], P(('pole', 'row'), 'col'), parts along dimension 0, may hold values from -0.12 to 0.12
- lower_third: float32 [4096, 512], P(('pole', 'row'), 'col'), parts along dimension 0, may hold values from -0.12 to 0.12
- ancestor: float32 [8, 3, 128, 128], P(('pole', 'col')), parts along dimension 0, may hold values from -0.6 to 0.6
- diag_inverse: float32 [6, 4, 128, 128], P('pole', 'col'), parts along dimension 0, may hold values from -1 to 2.5, as said below
- structure: int32 [4, 8], replicated, may hold values from 0 to 15, as said below
- pick_second: int32 [4, 7], replicated, may hold values from 0 to 7, as said below
- pick_third: int32 [4, 6], replicated, may hold values from 0 to 6, as said below
Outputs:
- first_cols: float32 [4096, 512], P(('pole', 'row'), 'col'), parts along dimension 0
- second_cols: float32 [4096, 512], P(('pole', 'row'), 'col'), parts along dimension 0
- third_cols: float32 [4096, 512], P(('pole', 'row'), 'col'), parts along dimension 0
- ancestral: float32 [8, 3, 128, 128], P(('pole', 'col')), parts along dimension 0
- diagonal: float32 [6, 4, 128, 128], P('pole', 'col'), parts along dimension 0
There are 2 independent parts, one for each index of `pole`. A program takes and returns all parts, laid end to end along the dimension named above; an argument that names none is the same for every part. Nothing has to cross between parts.
Inputs may be any that keep to these rules, and one draw needn't show every extreme that they name: `structure`: each row names 8 different separator blocks. `pick_second`: each row names 7 different positions. `pick_third`: each row names 6 different positions. `known_inverse`: exactly symmetric. Every block diag_inverse[l, k] is exactly symmetric.
All inputs are finite; a program needn't handle non-finite values.
Results may differ from a plain program's by a relative error of at most 0.000071.
Values sent between devices are 32-bit elements; how exact they have to be, the bound alone decides.
A program may use at most 128 MiB of HBM per device.

v0:
```python
import jax
import jax.numpy as jnp
from jax import lax
from jax.sharding import PartitionSpec as P

HIGHEST = lax.Precision.HIGHEST


def broadcast(array, axis, root):
    mine = lax.axis_index(axis) == root
    return lax.psum(jnp.where(mine, array, jnp.zeros_like(array)), axis)


def block_mask(members, block_count):
    block_ids = jnp.arange(block_count, dtype=jnp.int32)
    return jnp.sum((members[:, :, None] == block_ids[None, None, :]).astype(jnp.float32), axis=1)


def structure_masks(structure, pick_second, pick_third, block_count):
    second_ids = jnp.take_along_axis(structure, pick_second, axis=1)
    third_ids = jnp.take_along_axis(second_ids, pick_third, axis=1)
    return (
        block_mask(structure, block_count),
        block_mask(second_ids, block_count),
        block_mask(third_ids, block_count),
    )


def expand_mask(mask_table, block_size):
    return jnp.repeat(jnp.repeat(mask_table.T, block_size, axis=0), block_size, axis=1)


def node_times(columns, blocks):
    height = columns.shape[0]
    node_count = blocks.shape[0]
    block_size = blocks.shape[1]
    reshaped = columns.reshape(height, node_count, block_size)
    return jnp.einsum("rkb,kbc->rkc", reshaped, blocks, precision=HIGHEST).reshape(
        height, node_count * block_size
    )


def node_inner(former, latter, block_size):
    height = former.shape[0]
    node_count = former.shape[1] // block_size
    return jnp.einsum(
        "rkb,rkc->kbc",
        former.reshape(height, node_count, block_size),
        latter.reshape(height, node_count, block_size),
        precision=HIGHEST,
    )


def block_product(former, latter):
    return jnp.einsum("kbc,kcd->kbd", former, latter, precision=HIGHEST)


def block_tproduct(former, latter):
    return jnp.einsum("kcb,kcd->kbd", former, latter, precision=HIGHEST)


def row_total(partial_sum):
    return lax.psum(partial_sum, "row")


def on_device(
    known_inverse,
    lower_first,
    lower_second,
    lower_third,
    ancestor,
    diag_inverse,
    structure,
    pick_second,
    pick_third,
):
    block_size = ancestor.shape[2]
    row_group = lax.axis_size("row") // lax.axis_size("col")
    local_blocks = known_inverse.shape[0] // block_size
    block_count = local_blocks * lax.axis_size("row")
    local_nodes = ancestor.shape[0]
    masks = structure_masks(structure, pick_second, pick_third, block_count)
    block_start = lax.axis_index("row") * local_blocks
    node_start = lax.axis_index("col") * local_nodes
    expanded = [
        expand_mask(
            lax.dynamic_slice(mask_table, (node_start, block_start), (local_nodes, local_blocks)),
            block_size,
        )
        for mask_table in masks
    ]
    lowers = [
        factor * kept_rows
        for factor, kept_rows in zip((lower_first, lower_second, lower_third), expanded)
    ]
    products = []
    for masked in lowers:
        gathered = lax.all_gather(masked, "col", axis=1, tiled=True)
        pieces = [
            broadcast(gathered, "row", lax.axis_index("col") * row_group + offset)
            for offset in range(row_group)
        ]
        partial_value = jnp.dot(known_inverse, jnp.concatenate(pieces, axis=0), precision=HIGHEST)
        products.append(lax.psum_scatter(partial_value, "col", scatter_dimension=1, tiled=True))
    link_two = ancestor[:, 0]
    link_near = ancestor[:, 1]
    link_far = ancestor[:, 2]
    first_cols = -expanded[0] * products[0]
    diag_first = diag_inverse[0] - row_total(node_inner(lowers[0], first_cols, block_size))
    second_cols = -expanded[1] * (products[1] + node_times(first_cols, link_two))
    parent_part = lax.psum(node_inner(first_cols, lowers[1], block_size), "row")
    cross_two = -(parent_part + block_product(diag_first, link_two))
    diag_second = (
        diag_inverse[1]
        - row_total(node_inner(lowers[1], second_cols, block_size))
        - block_tproduct(link_two, cross_two)
    )
    third_cols = -expanded[2] * (
        products[2] + node_times(second_cols, link_near) + node_times(first_cols, link_far)
    )
    near_part, far_part = lax.psum(
        (
            node_inner(second_cols, lowers[2], block_size),
            node_inner(first_cols, lowers[2], block_size),
        ),
        "row",
    )
    cross_near = -(
        near_part + block_product(diag_second, link_near) + block_tproduct(cross_two, link_far)
    )
    cross_far = -(
        far_part + block_product(cross_two, link_near) + block_product(diag_first, link_far)
    )
    diag_third = (
        diag_inverse[2]
        - row_total(node_inner(lowers[2], third_cols, block_size))
        - block_tproduct(link_near, cross_near)
        - block_tproduct(link_far, cross_far)
    )
    ancestral = jnp.stack([cross_two, cross_near, cross_far], axis=1)
    diagonal = jnp.stack([diag_first, diag_second, diag_third], axis=0)
    return (first_cols, second_cols, third_cols, ancestral, diagonal)


def solution(mesh):
    placed = (
        P(("pole", "row"), "col"),
        P(("pole", "row"), "col"),
        P(("pole", "row"), "col"),
        P(("pole", "row"), "col"),
        P(("pole", "col"), None, None, None),
        P("pole", "col", None, None),
        P(),
        P(),
        P(),
    )
    return jax.shard_map(
        on_device,
        mesh=mesh,
        in_specs=placed,
        out_specs=(
            P(("pole", "row"), "col"),
            P(("pole", "row"), "col"),
            P(("pole", "row"), "col"),
            P(("pole", "col"), None, None, None),
            P("pole", "col", None, None),
        ),
        check_vma=False,
    )
```

profile of v0, /device:TPU:0, one launch (start us, length us, event | category | flops | bytes accessed | tf_op | source)
XLA Modules:
  0.0 315.6 jit_solution(9202363923579259804)
XLA Ops:
  16.3 29.4 %all-gather.8.cloned.1.call-done = f32[512,512]{1,0:T(8,128)} async-done(((f32[512,128]{1,0:T(8,128)}), f32[512,512]{1,0:T(8,128)}) %all-gather.8.cloned.1.call-update) | async-done | bytes 1048592 | tf_op jit(solution)/shard_map/all_gather | solution.py:98
  45.8 2.3 broadcast_select_fusion
  48.0 28.4 %all-gather.6.cloned.1.call-done = f32[512,512]{1,0:T(8,128)} async-done(((f32[512,128]{1,0:T(8,128)}), f32[512,512]{1,0:T(8,128)}) %all-gather.6.cloned.1.call-update) | async-done | bytes 1048592 | tf_op jit(solution)/shard_map/all_gather | solution.py:98
  76.4 2.3 broadcast_select_fusion.1
  78.7 28.4 %all-gather.4.cloned.1.call-done = f32[512,512]{1,0:T(8,128)} async-done(((f32[512,128]{1,0:T(8,128)}), f32[512,512]{1,0:T(8,128)}) %all-gather.4.cloned.1.call-update) | async-done | bytes 1048592 | tf_op jit(solution)/shard_map/all_gather | solution.py:98
  107.1 2.3 broadcast_select_fusion.2
  109.5 67.2 %all-reduce.7.cloned.1.call-done = (f32[512,512]{1,0:T(8,128)}, f32[512,512]{1,0:T(8,128)}, f32[512,512]{1,0:T(8,128)}) async-done(((f32[512,512]{1,0:T(8,128)}, f32[512,512]{1,0:T(8,128)}, f32[512,512]{1,0:T(8,128)}), (f32[512,512]{1,0:T(8,128)}, f32[512,512]{1,0:T(8,128)}, f32[512,512]{1,0:T(8,128)})) %all-reduce.7.cloned.1.call-update) | async-done | bytes 3145744 | tf_op jit(solution)/shard_map/psum | solution.py:11
  176.7 5.7 %convolution_bitcast_fusion.2 = f32[512,512]{0,1:T(8,128)} fusion(f32[512,512]{1,0:T(8,128)} %get-tuple-element.26, f32[512,512]{1,0:T(8,128)S(1)} %copy-done), kind=kOutput, calls=%fused_computation.4 | convolution fusion | flops 1610612736 | bytes 3145728 | tf_op jit(solution)/shard_map/dot_general | solution.py:103
  182.4 1.1 copy-done.7
  183.6 4.5 %convolution_bitcast_fusion.1 = f32[512,512]{0,1:T(8,128)} fusion(f32[512,512]{1,0:T(8,128)S(1)} %copy-done.7, f32[512,512]{1,0:T(8,128)S(1)} %copy-done), kind=kOutput, calls=%fused_computation.3 | convolution fusion | flops 1610612736 | bytes 3145728 | tf_op jit(solution)/shard_map/dot_general | solution.py:103
  188.1 1.2 copy-done.6
  189.3 4.5 %convolution_bitcast_fusion = f32[512,512]{0,1:T(8,128)} fusion(f32[512,512]{1,0:T(8,128)S(1)} %copy-done.6, f32[512,512]{1,0:T(8,128)S(1)} %copy-done), kind=kOutput, calls=%fused_computation.2 | convolution fusion | flops 1610612736 | bytes 3145728 | tf_op jit(solution)/shard_map/dot_general | solution.py:103
  194.3 15.5 %reduce-scatter.4.cloned.1.call-done = f32[512,128]{0,1:T(8,128)} async-done(((f32[512,512]{0,1:T(8,128)}), f32[512,128]{0,1:T(8,128)}) %reduce-scatter.4.cloned.1.call-update) | async-done | bytes 262160 | tf_op jit(solution)/shard_map/reduce_scatter | solution.py:104
  210.8 27.1 %reduce-scatter.6.cloned.1.call-done = f32[512,128]{0,1:T(8,128)} async-done(((f32[512,512]{0,1:T(8,128)}), f32[512,128]{0,1:T(8,128)}) %reduce-scatter.6.cloned.1.call-update) | async-done | bytes 262160 | tf_op jit(solution)/shard_map/reduce_scatter | solution.py:104
  237.8 1.4 fusion.1
  239.2 1.2 convolution_bitcast_fusion.13
  240.4 1.0 convolution_bitcast_fusion.14
  241.5 1.0 convolution_bitcast_fusion.12
  243.5 1.2 convolution_bitcast_fusion.15
  244.7 21.3 %reduce-scatter.8.cloned.1.call-done = f32[512,128]{0,1:T(8,128)} async-done(((f32[512,512]{0,1:T(8,128)}), f32[512,128]{0,1:T(8,128)}) %reduce-scatter.8.cloned.1.call-update) | async-done | bytes 262160 | tf_op jit(solution)/shard_map/reduce_scatter | solution.py:104
  266.0 1.4 convolution_add_fusion.1
  267.8 1.2 convolution_bitcast_fusion.11
  271.5 29.8 %all-reduce.5.cloned.1.call-done = (f32[1,128,128]{2,1,0:T(8,128)}, f32[1,128,128]{2,1,0:T(8,128)}, f32[1,128,128]{2,1,0:T(8,128)}, f32[1,128,128]{2,1,0:T(8,128...) async-done(((f32[1,128,128]{2,1,0:T(8,128)}, f32[1,128,128]{2,1,0:T(8,128)}, f32[1,128,128]{2,1,0:T(8,128)}, f32[1,128,128]{2,1,0:T(8,128)}, f32[1,128,128]{2,1,0:T(8,128)}, ...) | async-done | bytes 393232 | tf_op jit(solution)/shard_map/psum | solution.py:63
  301.3 1.1 convolution_bitcast_fusion.5
  (96 shorter events, 20.9 us)
Async XLA Ops:
  7.2 169.5 %copy-start = (f32[512,512]{1,0:T(8,128)S(1)}, f32[512,512]{1,0:T(8,128)}, u32[]{:S(2)}) copy-start(f32[512,512]{1,0:T(8,128)} %param.9) | copy-start | bytes 3145732
  7.2 38.6 %all-gather.8.cloned.1.call-start = ((), (), s32[]{:S(2)}) async-start(), calls=%async_computation.7 | async-start | bytes 1310720 | tf_op jit(solution)/shard_map/all_gather | solution.py:98
  10.5 1.4 copy-start.10
  12.7 0.9 copy-start.11
  12.7 63.7 %all-gather.6.cloned.1.call-start = ((), (), s32[]{:S(2)}) async-start(), calls=%async_computation.5 | async-start | bytes 1310720 | tf_op jit(solution)/shard_map/all_gather | solution.py:98
  14.5 0.9 copy-start.12
  14.5 92.6 %all-gather.4.cloned.1.call-start = ((), (), s32[]{:S(2)}) async-start(), calls=%async_computation.3 | async-start | bytes 1310720 | tf_op jit(solution)/shard_map/all_gather | solution.py:98
  16.3 160.4 %all-reduce.7.cloned.1.call-start = ((), (), s32[]{:S(2)}) async-start(), calls=%async_computation.10 | async-start | bytes 6291456 | tf_op jit(solution)/shard_map/psum | solution.py:11
  109.4 100.3 %reduce-scatter.4.cloned.1.call-start = ((), (), s32[]{:S(2)}) async-start(), calls=%async_computation.4 | async-start | bytes 1310720 | tf_op jit(solution)/shard_map/reduce_scatter | solution.py:104
  182.4 1.2 copy-start.7
  182.4 55.5 %reduce-scatter.6.cloned.1.call-start = ((), (), s32[]{:S(2)}) async-start(), calls=%async_computation.6 | async-start | bytes 1310720 | tf_op jit(solution)/shard_map/reduce_scatter | solution.py:104
  188.0 1.3 copy-start.6
  188.1 77.9 %reduce-scatter.8.cloned.1.call-start = ((), (), s32[]{:S(2)}) async-start(), calls=%async_computation.8 | async-start | bytes 1310720 | tf_op jit(solution)/shard_map/reduce_scatter | solution.py:104
  193.8 107.5 %all-reduce.5.cloned.1.call-start = ((), (), s32[]{:S(2)}) async-start(), calls=%async_computation.9 | async-start | bytes 786432 | tf_op jit(solution)/shard_map/psum | solution.py:63
  194.3 43.6 %copy-start.4 = (f32[1,3,128,128]{3,2,1,0:T(8,128)S(1)}, f32[1,3,128,128]{3,2,1,0:T(8,128)}, u32[]{:S(2)}) copy-start(f32[1,3,128,128]{3,2,1,0:T(8,128)} %param.13) | copy-start | bytes 589828
  210.7 28.5 %copy-start.3 = (f32[512,128]{1,0:T(8,128)S(1)}, f32[512,128]{1,0:T(8,128)}, u32[]{:S(2)}) copy-start(f32[512,128]{1,0:T(8,128)} %broadcast_multiply_fusion.1) | copy-start | bytes 786436
  239.2 1.2 copy-start.2
  242.5 1.0 copy-start.5
  270.7 30.7 %copy-start.9 = (f32[3,1,128,128]{3,2,1,0:T(8,128)S(1)}, f32[3,1,128,128]{3,2,1,0:T(8,128)}, u32[]{:S(2)}) copy-start(f32[3,1,128,128]{3,2,1,0:T(8,128)} %param.14) | copy-start | bytes 589828
  301.3 1.1 copy-start.8
  302.5 0.8 copy-start.17
  303.5 0.8 copy-start.16
  304.3 0.8 copy-start.15
  305.2 0.8 copy-start.14
  (4 other events, 3.0 us)
Sparse Core Ops, SparseCore 0:
  12.8 32.8 all-gather.7
  47.9 28.4 all-gather.5
  78.6 28.4 all-gather.3
  109.6 67.0 all-reduce.6
  182.5 27.2 reduce-scatter.3
  212.0 25.7 reduce-scatter.5
  240.1 25.7 reduce-scatter.7
  269.5 31.7 all-reduce.4
where the time goes:
time: 316 us
  waiting for transfers between devices  247 us (78%)
  matrix products  27.3 us (9%)
  between operations  14.4 us (5%)
  local copies, waits for them, and re-layouts  14 us (4%)
  other arithmetic  12.2 us (4%)
    all_gather x3, waiting for transfers between devices, on_device(): gathered = lax.all_gather(masked, 'col', axis=1, tiled=True)  86.2 us
    psum x1, waiting for transfers between devices, broadcast(): return lax.psum(jnp.where(mine, array, jnp.zeros_like(array)), axis)  67.2 us
    reduce_scatter x3, waiting for transfers between devices, on_device(): lax.psum_scatter(partial_value, 'col', scatter_dimension=1, tiled=True)  63.8 us
    psum x1, waiting for transfers between devices, row_total(): return lax.psum(partial_sum, 'row')  29.8 us
    dot_general x3, matrix products, on_device(): jnp.dot(known_inverse, jnp.concatenate(pieces, axis=0), precision=HIGHEST)  14.6 us
    unnamed x43, local copies, waits for them, and re-layouts  11.4 us
    select_n x3, other arithmetic, broadcast(): return lax.psum(jnp.where(mine, array, jnp.zeros_like(array)), axis)  6.87 us
    dot_general x6, matrix products, node_inner(): jnp.einsum('rkb,rkc->kbc', former.reshape(height, node_count, block_size)...  6.68 us
  transfers between devices with their start and end apart: 8, of which 8 were waited for; matrix products, arithmetic and copies ran while one was open for 8% of the time, Pallas kernels for 0%

commit v1 on v0

--- a/solution.py
+++ b/solution.py
@@ -1,6 +1,8 @@
 import jax
 import jax.numpy as jnp
 from jax import lax
+from jax.experimental import pallas as pl
+from jax.experimental.pallas import tpu as pltpu
 from jax.sharding import PartitionSpec as P
 
 HIGHEST = lax.Precision.HIGHEST
@@ -142,7 +144,393 @@
     return (first_cols, second_cols, third_cols, ancestral, diagonal)
 
 
+SIDE = 4
+BLOCK = 128
+CHUNKS = 8
+MESH = pl.DeviceIdType.MESH
+
+
+def landing_plan():
+    half = {
+        (0, 0): [],
+        (1, 0): [(2, 2, False), (3, 3, False), (1, 1, True)],
+        (2, 0): [(2, 1, False)],
+        (3, 0): [(2, 1, False), (3, 1, False)],
+        (0, 1): [(0, 0, False)],
+        (1, 1): [],
+        (2, 1): [(0, 0, False), (2, 2, False)],
+        (3, 1): [(0, 0, False), (2, 2, False), (3, 3, False)],
+    }
+    plan = {}
+    for (row, col), slots in half.items():
+        plan[row, col] = [(col, None, False)] + slots
+        plan[3 - row, 3 - col] = [(3 - col, None, False)] + [
+            (3 - other, 3 - source, late) for other, source, late in slots
+        ]
+    return plan
+
+
+def transfers():
+    plan = landing_plan()
+    sends = {place: [] for place in plan}
+    for (row, col), slots in plan.items():
+        for slot, (other, source, late) in enumerate(slots):
+            if slot == 0:
+                continue
+            held = [have[0] for have in plan[row, source]]
+            assert other in held
+            sends[row, source].append((held.index(other), (row, col), slot, late))
+    return plan, sends
+
+
+def lookup(me, values):
+    total = jnp.int32(0)
+    for place, value in values.items():
+        if value:
+            total = total + jnp.where(me == place[0] * SIDE + place[1], jnp.int32(value), jnp.int32(0))
+    return total
+
+
+def split(value):
+    high = value.astype(jnp.bfloat16)
+    low = (value - high.astype(jnp.float32)).astype(jnp.bfloat16)
+    return high, low
+
+
+def mul(a, b):
+    return jnp.dot(a, b, preferred_element_type=jnp.float32)
+
+
+def dot3(left, right):
+    return mul(left[0], right[0]) + (mul(left[0], right[1]) + mul(left[1], right[0]))
+
+
+def fused_kernel(
+    structure_ref, second_ref, third_ref,
+    k_ref, l1_ref, l2_ref, l3_ref, anc_ref, dinv_ref,
+    first_ref, second_out, third_out, ancestral_ref, diagonal_ref,
+    kbuf, mf, mhi, mlo, acc, outm, pin, part, got_core, half_sum, got_row, total,
+    ksend, krecv, msend, mrecv, psend, precv, rsend, rrecv,
+):
+    row = lax.axis_index("row")
+    col = lax.axis_index("col")
+    me = row * SIDE + col
+    plan, sends = transfers()
+    levels = (l1_ref, l2_ref, l3_ref)
+    rows_of = SIDE * BLOCK
+    step_rows = rows_of // CHUNKS
+
+    def at(place):
+        return pl.when(me == place[0] * SIDE + place[1])
+
+    def block_copy(index, source_slot, target, slot, chunk):
+        rows = pl.ds(chunk * step_rows, step_rows)
+        source = k_ref.at[rows] if source_slot == 0 else kbuf.at[source_slot - 1, rows]
+        return pltpu.make_async_remote_copy(
+            src_ref=source,
+            dst_ref=kbuf.at[slot - 1, rows],
+            send_sem=ksend.at[index, chunk],
+            recv_sem=krecv.at[slot - 1, chunk],
+            device_id={"col": target[1]},
+            device_id_type=MESH,
+        )
+
+    def wait_block(slot, chunk):
+        rows = pl.ds(chunk * step_rows, step_rows)
+        pltpu.make_async_copy(k_ref.at[rows], kbuf.at[slot - 1, rows], krecv.at[slot - 1, chunk]).wait()
+
+    def factor_copy(owner, taker):
+        return pltpu.make_async_remote_copy(
+            src_ref=mf.at[owner],
+            dst_ref=mf.at[owner],
+            send_sem=msend.at[taker],
+            recv_sem=mrecv.at[owner],
+            device_id={"row": taker},
+            device_id_type=MESH,
+        )
+
+    def product_copy(sender, slot, taker):
+        return pltpu.make_async_remote_copy(
+            src_ref=outm.at[slot],
+            dst_ref=pin.at[sender],
+            send_sem=psend.at[slot],
+            recv_sem=precv.at[sender],
+            device_id={"row": taker},
+            device_id_type=MESH,
+        )
+
+    barrier = pltpu.get_barrier_semaphore()
+    for step in range(1, SIDE):
+        pl.semaphore_signal(barrier, inc=1, device_id={"col": lax.rem(col + step, SIDE)}, device_id_type=MESH)
+        pl.semaphore_signal(barrier, inc=1, device_id={"row": lax.rem(row + step, SIDE)}, device_id_type=MESH)
+    pl.semaphore_wait(barrier, 2 * (SIDE - 1))
+
+    for place, listed in sends.items():
+        early = [(i, s) for i, s in enumerate(listed) if s[0] == 0 and not s[3]]
+        if early:
+            @at(place)
+            def _(early=early):
+                for chunk in range(CHUNKS):
+                    for index, (source_slot, target, slot, _) in early:
+                        block_copy(index, source_slot, target, slot, chunk).start()
+
+    def marks(ids, block):
+        total_mark = jnp.float32(0)
+        for one in ids:
+            total_mark = total_mark + jnp.where(one == block, jnp.float32(1), jnp.float32(0))
+        return total_mark
+
+    ids_1 = [structure_ref[col, i] for i in range(structure_ref.shape[1])]
+    ids_2 = [structure_ref[col, second_ref[col, i]] for i in range(second_ref.shape[1])]
+    ids_3 = [
+        structure_ref[col, second_ref[col, third_ref[col, i]]] for i in range(third_ref.shape[1])
+    ]
+    keep = [[marks(ids, row * SIDE + i) for i in range(SIDE)] for ids in (ids_1, ids_2, ids_3)]
+    for level in range(3):
+        for i in range(SIDE):
+            rows = slice(i * BLOCK, (i + 1) * BLOCK)
+            columns = slice(level * BLOCK, (level + 1) * BLOCK)
+            mf[row, rows, columns] = levels[level][rows, :] * keep[level][i]
+
+    needs = {place: [] for place in plan}
+    for (r, k), slots in plan.items():
+        for slot, (other, _, _) in enumerate(slots):
+            if other != r:
+                needs[other, k].append((slot, r))
+    for (b, k), takers in needs.items():
+        if takers:
+            @at((b, k))
+            def _(b=b, takers=takers):
+                for _, taker in sorted(takers):
+                    factor_copy(b, taker).start()
+
+    acc[...] = jnp.zeros_like(acc)
+
+    def split_factor(index):
+        def body(t, carry):
+            rows = pl.ds(pl.multiple_of(t * BLOCK, BLOCK), BLOCK)
+            high, low = split(mf[index, rows, :])
+            mhi[index, rows, :] = high
+            mlo[index, rows, :] = low
+            return carry
+        lax.fori_loop(0, SIDE, body, 0)
+
+    split_factor(row)
+
+    def relay(chunks):
+        for place, listed in sends.items():
+            passed = [(i, s) for i, s in enumerate(listed) if s[0] != 0]
+            if passed:
+                @at(place)
+                def _(passed=passed):
+                    for chunk in chunks:
+                        for index, (source_slot, target, slot, _) in passed:
+                            wait_block(source_slot, chunk)
+                            block_copy(index, source_slot, target, slot, chunk).start()
+
+    relay(range(0, CHUNKS // 2))
+
+    def work(slot):
+        has = lookup(me, {p: int(len(s) > slot) for p, s in plan.items()})
+        other = lookup(me, {p: s[slot][0] for p, s in plan.items() if len(s) > slot})
+        source = k_ref if slot == 0 else kbuf.at[slot - 1]
+        if slot > 0:
+            relayed = {
+                p: int(any(s[0] == slot for s in listed)) for p, listed in sends.items()
+            }
+            fresh = has - lookup(me, relayed)
+
+            @pl.when(fresh == 1)
+            def _():
+                for chunk in range(CHUNKS):
+                    wait_block(slot, chunk)
+
+        @pl.when((has == 1) & (other != row))
+        def _():
+            pltpu.make_async_copy(mf.at[other], mf.at[other], mrecv.at[other]).wait()
+            split_factor(other)
+            def body(t, carry):
+                part_of = pl.ds(pl.multiple_of(t * BLOCK, BLOCK), BLOCK)
+                turned = split(source[:, part_of].T)
+                outm[slot, part_of, :] = dot3(turned, (mhi[row], mlo[row]))
+                return carry
+            lax.fori_loop(0, SIDE, body, 0)
+
+        for place, slots in plan.items():
+            if len(slots) > slot and slots[slot][0] != place[0]:
+                @at(place)
+                def _(place=place, taker=slots[slot][0]):
+                    product_copy(place[0], slot, taker).start()
+
+        @pl.when(has == 1)
+        def _():
+            def body(t, carry):
+                part_of = pl.ds(pl.multiple_of(t * BLOCK, BLOCK), BLOCK)
+                straight = split(source[part_of, :])
+                acc[part_of, :] += dot3(straight, (mhi[other], mlo[other]))
+                return carry
+            lax.fori_loop(0, SIDE, body, 0)
+
+    work(0)
+    for place, listed in sends.items():
+        late = [(i, s) for i, s in enumerate(listed) if s[3]]
+        if late:
+            @at(place)
+            def _(late=late):
+                for chunk in range(CHUNKS):
+                    for index, (source_slot, target, slot, _) in late:
+                        block_copy(index, source_slot, target, slot, chunk).start()
+    relay(range(CHUNKS // 2, CHUNKS))
+    for slot in range(1, SIDE):
+        work(slot)
+
+    for sender in range(SIDE):
+        gets = lookup(me, {
+            p: 1 for p in plan
+            if p[0] != sender and any(s[0] == p[0] for s in plan[sender, p[1]])
+        })
+
+        @pl.when(gets == 1)
+        def _(sender=sender):
+            pltpu.make_async_copy(outm.at[0], pin.at[sender], precv.at[sender]).wait()
+            acc[...] += pin[sender]
+
+    def kept(value, level):
+        return jnp.concatenate(
+            [-(value[i * BLOCK:(i + 1) * BLOCK, :] * keep[level][i]) for i in range(SIDE)], axis=0
+        )
+
+    factors = (mhi[row], mlo[row])
+    links = [split(anc_ref[0, i]) for i in range(3)]
+    first = kept(acc[:, 0:BLOCK], 0)
+    first_ref[...] = first
+    first_split = split(first)
+    inner_first = dot3(split(first.T), factors)
+    part[0, 0] = inner_first[:, 0:BLOCK].T
+    part[0, 1] = inner_first[:, BLOCK:2 * BLOCK]
+    part[0, 2] = inner_first[:, 2 * BLOCK:]
+    second = kept(acc[:, BLOCK:2 * BLOCK] + dot3(first_split, links[0]), 1)
+    second_out[...] = second
+    later = (factors[0][:, BLOCK:], factors[1][:, BLOCK:])
+    inner_second = dot3(split(second.T), later)
+    part[1, 0] = inner_second[:, 0:BLOCK].T
+    part[1, 1] = inner_second[:, BLOCK:]
+    third = kept(
+        acc[:, 2 * BLOCK:] + dot3(split(second), links[1]) + dot3(first_split, links[2]), 2
+    )
+    third_out[...] = third
+    last = (factors[0][:, 2 * BLOCK:], factors[1][:, 2 * BLOCK:])
+    part[1, 2] = dot3(split(third.T), last).T
+
+    mine = lax.rem(row, 2)
+    sibling = row + 1 - 2 * mine
+    across = lax.rem(row + 2, SIDE)
+
+    def exchange(source, target, index, partner):
+        copy = pltpu.make_async_remote_copy(
+            src_ref=source,
+            dst_ref=target,
+            send_sem=rsend.at[index],
+            recv_sem=rrecv.at[index],
+            device_id={"row": partner},
+            device_id_type=MESH,
+        )
+        copy.start()
+        return copy
+
+    copy = exchange(part.at[1 - mine], got_core, 0, sibling)
+    copy.wait()
+    half_sum[...] = part[mine] + got_core[...]
+    copy = exchange(half_sum, got_row, 1, across)
+    copy.wait()
+    total[mine] = half_sum[...] + got_row[...]
+    copy = exchange(total.at[mine], total.at[mine], 2, sibling)
+    copy.wait()
+
+    turned = [split(anc_ref[0, i].T) for i in range(3)]
+    diag_1 = dinv_ref[0, 0] - total[0, 0]
+    diag_1s = split(diag_1)
+    cross = -(total[0, 1] + dot3(diag_1s, links[0]))
+    cross_s = split(cross)
+    diag_2 = dinv_ref[1, 0] - total[1, 0] - dot3(turned[0], cross_s)
+    near = -(total[1, 1] + dot3(split(diag_2), links[1]) + dot3(split(cross.T), links[2]))
+    far = -(total[0, 2] + dot3(cross_s, links[1]) + dot3(diag_1s, links[2]))
+    diag_3 = dinv_ref[2, 0] - total[1, 2] - dot3(turned[1], split(near)) - dot3(turned[2], split(far))
+    ancestral_ref[0, 0] = cross
+    ancestral_ref[0, 1] = near
+    ancestral_ref[0, 2] = far
+    diagonal_ref[0, 0] = diag_1
+    diagonal_ref[1, 0] = diag_2
+    diagonal_ref[2, 0] = diag_3
+
+    for place, listed in sends.items():
+        @at(place)
+        def _(place=place, listed=listed):
+            for index, (source_slot, target, slot, _) in enumerate(listed):
+                for chunk in range(CHUNKS):
+                    block_copy(index, source_slot, target, slot, chunk).wait_send()
+            for _, taker in needs[place]:
+                factor_copy(place[0], taker).wait_send()
+            for slot, (other, _, _) in enumerate(plan[place]):
+                if other != place[0]:
+                    product_copy(place[0], slot, other).wait_send()
+
+
+def on_device_fused(
+    known_inverse, lower_first, lower_second, lower_third, ancestor, diag_inverse,
+    structure, pick_second, pick_third,
+):
+    rows = SIDE * BLOCK
+    wide = 3 * BLOCK
+    f32 = jnp.float32
+    most = max(len(listed) for listed in transfers()[1].values())
+    smem = pl.BlockSpec(memory_space=pltpu.SMEM)
+    vmem = pl.BlockSpec(memory_space=pltpu.VMEM)
+    dma = pltpu.SemaphoreType.DMA
+    return pl.pallas_call(
+        fused_kernel,
+        out_shape=(
+            jax.ShapeDtypeStruct((rows, BLOCK), f32),
+            jax.ShapeDtypeStruct((rows, BLOCK), f32),
+            jax.ShapeDtypeStruct((rows, BLOCK), f32),
+            jax.ShapeDtypeStruct((1, 3, BLOCK, BLOCK), f32),
+            jax.ShapeDtypeStruct((3, 1, BLOCK, BLOCK), f32),
+        ),
+        in_specs=[smem] * 3 + [vmem] * 6,
+        out_specs=[vmem] * 5,
+        scratch_shapes=[
+            pltpu.VMEM((SIDE - 1, rows, rows), f32),
+            pltpu.VMEM((SIDE, rows, wide), f32),
+            pltpu.VMEM((SIDE, rows, wide), jnp.bfloat16),
+            pltpu.VMEM((SIDE, rows, wide), jnp.bfloat16),
+            pltpu.VMEM((rows, wide), f32),
+            pltpu.VMEM((SIDE, rows, wide), f32),
+            pltpu.VMEM((SIDE, rows, wide), f32),
+            pltpu.VMEM((2, 3, BLOCK, BLOCK), f32),
+            pltpu.VMEM((3, BLOCK, BLOCK), f32),
+            pltpu.VMEM((3, BLOCK, BLOCK), f32),
+            pltpu.VMEM((3, BLOCK, BLOCK), f32),
+            pltpu.VMEM((2, 3, BLOCK, BLOCK), f32),
+            dma((most, CHUNKS)),
+            dma((SIDE - 1, CHUNKS)),
+            dma((SIDE,)),
+            dma((SIDE,)),
+            dma((SIDE,)),
+            dma((SIDE,)),
+            dma((3,)),
+            dma((3,)),
+        ],
+        compiler_params=pltpu.CompilerParams(
+            collective_id=0, has_side_effects=True, vmem_limit_bytes=40 * 1024 * 1024
+        ),
+    )(
+        structure, pick_second, pick_third, known_inverse, lower_first, lower_second, lower_third,
+        ancestor, diag_inverse,
+    )
+
+
 def solution(mesh):
+    fused = mesh.shape["row"] == SIDE and mesh.shape["col"] == SIDE
     placed = (
         P(("pole", "row"), "col"),
         P(("pole", "row"), "col"),
@@ -155,7 +543,7 @@
         P(),
     )
     return jax.shard_map(
-        on_device,
+        on_device_fused if fused else on_device,
         mesh=mesh,
         in_specs=placed,
         out_specs=(

time: 316 us -> 93.5 us (0.30)
  the two profiles are of different devices: /device:TPU:0 before, /device:TPU:19 now
where the time goes in v1:
time: 93.5 us; the launch traced here: 93.1 us
  Pallas kernels  81 us (87%)
  local copies, waits for them, and re-layouts  11.4 us (12%)
    pallas_call x1, Pallas kernels, on_device_fused(): pl.pallas_call(fused_kernel, out_shape=(jax.ShapeDtypeStruct((rows, BLOCK...  81 us
    unnamed x23, local copies, waits for them, and re-layouts  11.4 us

profile of v1, /device:TPU:19, one launch (start us, length us, event | category | flops | bytes accessed | tf_op | source)
XLA Modules:
  0.0 93.1 jit_solution(4187985301443830522)
XLA Ops:
  0.6 0.0 copy-start
  0.6 1.2 %copy-done = f32[512,512]{1,0:T(8,128)S(1)} copy-done((f32[512,512]{1,0:T(8,128)S(1)}, f32[512,512]{1,0:T(8,128)}, u32[]{:S(2)}) %copy-start) | copy-done | bytes 1048600
  1.9 0.0 copy-start.1
  1.9 0.9 %copy-done.1 = f32[512,128]{1,0:T(8,128)S(1)} copy-done((f32[512,128]{1,0:T(8,128)S(1)}, f32[512,128]{1,0:T(8,128)}, u32[]{:S(2)}) %copy-start.1) | copy-done | bytes 262168
  2.8 0.0 copy-start.2
  2.8 0.9 %copy-done.2 = f32[512,128]{1,0:T(8,128)S(1)} copy-done((f32[512,128]{1,0:T(8,128)S(1)}, f32[512,128]{1,0:T(8,128)}, u32[]{:S(2)}) %copy-start.2) | copy-done | bytes 262168
  3.8 0.0 copy-start.3
  3.8 0.9 %copy-done.3 = f32[512,128]{1,0:T(8,128)S(1)} copy-done((f32[512,128]{1,0:T(8,128)S(1)}, f32[512,128]{1,0:T(8,128)}, u32[]{:S(2)}) %copy-start.3) | copy-done | bytes 262168
  4.7 0.0 copy-start.4
  4.7 0.9 copy-done.4
  5.6 0.0 copy-start.5
  5.6 0.9 copy-done.5
  6.6 0.0 copy-start.6
  6.6 0.7 copy-done.6
  7.2 0.0 copy-start.7
  7.3 0.7 copy-done.7
  7.9 0.0 copy-start.8
  7.9 0.7 copy-done.8
  8.6 81.0 %shard_map.128 = (f32[512,128]{1,0:T(8,128)S(1)}, f32[512,128]{1,0:T(8,128)S(1)}, f32[512,128]{1,0:T(8,128)S(1)}, f32[1,3,128,128]{3,2,1,0:T(8,128)S(1)}, f32[3,1,128,128]{3,2,1,0:T(8,128)S(1)}) custom-call(s32[4,8]{1,0:T(4,128)S(1)} %copy-done.6, s32[4,7]{1,0:T(4,128)S(1)} %copy-done.7, s32[4,6]{1,0:T(4,128)S(1)} %copy-done.8, f32[512,512]{1,0:T(8,128)S(1)} %copy-done, ...), custom_call_target="tpu_custom_call" | custom-call | tf_op jit(solution)/shard_map/pallas_call | solution.py:490
  89.6 0.7 copy.19
  90.3 0.7 copy.20
  91.0 0.7 copy.21
  91.7 0.7 copy.22
  92.4 0.7 copy.23
Async XLA Ops:
  0.6 1.2 %copy-start = (f32[512,512]{1,0:T(8,128)S(1)}, f32[512,512]{1,0:T(8,128)}, u32[]{:S(2)}) copy-start(f32[512,512]{1,0:T(8,128)} %k_ref.1) | copy-start | bytes 3145732
  1.9 0.9 %copy-start.1 = (f32[512,128]{1,0:T(8,128)S(1)}, f32[512,128]{1,0:T(8,128)}, u32[]{:S(2)}) copy-start(f32[512,128]{1,0:T(8,128)} %l1_ref.1) | copy-start | bytes 786436
  2.8 0.9 %copy-start.2 = (f32[512,128]{1,0:T(8,128)S(1)}, f32[512,128]{1,0:T(8,128)}, u32[]{:S(2)}) copy-start(f32[512,128]{1,0:T(8,128)} %l2_ref.1) | copy-start | bytes 786436
  3.8 0.9 %copy-start.3 = (f32[512,128]{1,0:T(8,128)S(1)}, f32[512,128]{1,0:T(8,128)}, u32[]{:S(2)}) copy-start(f32[512,128]{1,0:T(8,128)} %l3_ref.1) | copy-start | bytes 786436
  4.7 0.9 copy-start.4
  5.6 0.9 copy-start.5
  6.6 0.7 copy-start.6
  7.2 0.7 copy-start.7
  7.9 0.7 copy-start.8

commit v2 on v1

--- a/solution.py
+++ b/solution.py
@@ -153,7 +153,7 @@
 def landing_plan():
     half = {
         (0, 0): [],
-        (1, 0): [(2, 2, False), (3, 3, False), (1, 1, True)],
+        (1, 0): [(2, 2, False), (3, 3, True), (1, 1, True)],
         (2, 0): [(2, 1, False)],
         (3, 0): [(2, 1, False), (3, 1, False)],
         (0, 1): [(0, 0, False)],
@@ -206,9 +206,9 @@
 
 
 def fused_kernel(
-    structure_ref, second_ref, third_ref,
-    k_ref, l1_ref, l2_ref, l3_ref, anc_ref, dinv_ref,
+    structure_in, second_in, third_in, k_ref, l1_in, l2_in, l3_in, anc_in, dinv_in,
     first_ref, second_out, third_out, ancestral_ref, diagonal_ref,
+    structure_ref, second_ref, third_ref, lbuf, anc_ref, dinv_ref, copied,
     kbuf, mf, mhi, mlo, acc, outm, pin, part, got_core, half_sum, got_row, total,
     ksend, krecv, msend, mrecv, psend, precv, rsend, rrecv,
 ):
@@ -216,7 +216,6 @@
     col = lax.axis_index("col")
     me = row * SIDE + col
     plan, sends = transfers()
-    levels = (l1_ref, l2_ref, l3_ref)
     rows_of = SIDE * BLOCK
     step_rows = rows_of // CHUNKS
 
@@ -225,10 +224,10 @@
 
     def block_copy(index, source_slot, target, slot, chunk):
         rows = pl.ds(chunk * step_rows, step_rows)
-        source = k_ref.at[rows] if source_slot == 0 else kbuf.at[source_slot - 1, rows]
+        source = k_ref.at[rows] if source_slot == 0 else kbuf.at[source_slot, rows]
         return pltpu.make_async_remote_copy(
             src_ref=source,
-            dst_ref=kbuf.at[slot - 1, rows],
+            dst_ref=kbuf.at[slot, rows],
             send_sem=ksend.at[index, chunk],
             recv_sem=krecv.at[slot - 1, chunk],
             device_id={"col": target[1]},
@@ -237,7 +236,7 @@
 
     def wait_block(slot, chunk):
         rows = pl.ds(chunk * step_rows, step_rows)
-        pltpu.make_async_copy(k_ref.at[rows], kbuf.at[slot - 1, rows], krecv.at[slot - 1, chunk]).wait()
+        pltpu.make_async_copy(k_ref.at[rows], kbuf.at[slot, rows], krecv.at[slot - 1, chunk]).wait()
 
     def factor_copy(owner, taker):
         return pltpu.make_async_remote_copy(
@@ -259,6 +258,17 @@
             device_id_type=MESH,
         )
 
+    local = [
+        pltpu.make_async_copy(source, target, copied.at[index])
+        for index, (source, target) in enumerate([
+            (structure_in, structure_ref), (second_in, second_ref), (third_in, third_ref),
+            (l1_in, lbuf.at[0]), (l2_in, lbuf.at[1]), (l3_in, lbuf.at[2]),
+            (k_ref, kbuf.at[0]), (anc_in, anc_ref), (dinv_in, dinv_ref),
+        ])
+    ]
+    for copy in local:
+        copy.start()
+
     barrier = pltpu.get_barrier_semaphore()
     for step in range(1, SIDE):
         pl.semaphore_signal(barrier, inc=1, device_id={"col": lax.rem(col + step, SIDE)}, device_id_type=MESH)
@@ -273,6 +283,9 @@
                 for chunk in range(CHUNKS):
                     for index, (source_slot, target, slot, _) in early:
                         block_copy(index, source_slot, target, slot, chunk).start()
+
+    for copy in local[:6]:
+        copy.wait()
 
     def marks(ids, block):
         total_mark = jnp.float32(0)
@@ -290,7 +303,7 @@
         for i in range(SIDE):
             rows = slice(i * BLOCK, (i + 1) * BLOCK)
             columns = slice(level * BLOCK, (level + 1) * BLOCK)
-            mf[row, rows, columns] = levels[level][rows, :] * keep[level][i]
+            mf[row, rows, columns] = lbuf[level, rows, :] * keep[level][i]
 
     needs = {place: [] for place in plan}
     for (r, k), slots in plan.items():
@@ -328,30 +341,29 @@
                             wait_block(source_slot, chunk)
                             block_copy(index, source_slot, target, slot, chunk).start()
 
-    relay(range(0, CHUNKS // 2))
-
-    def work(slot):
-        has = lookup(me, {p: int(len(s) > slot) for p, s in plan.items()})
-        other = lookup(me, {p: s[slot][0] for p, s in plan.items() if len(s) > slot})
-        source = k_ref if slot == 0 else kbuf.at[slot - 1]
-        if slot > 0:
-            relayed = {
-                p: int(any(s[0] == slot for s in listed)) for p, listed in sends.items()
-            }
-            fresh = has - lookup(me, relayed)
-
-            @pl.when(fresh == 1)
-            def _():
-                for chunk in range(CHUNKS):
-                    wait_block(slot, chunk)
-
-        @pl.when((has == 1) & (other != row))
+    for copy in local[6:]:
+        copy.wait()
+
+    has_slot = [lookup(me, {p: int(len(s) > slot) for p, s in plan.items()}) for slot in range(SIDE)]
+    other_of = [
+        lookup(me, {p: s[slot][0] for p, s in plan.items() if len(s) > slot}) for slot in range(SIDE)
+    ]
+
+    def arrive(slot):
+        relayed = {p: int(any(s[0] == slot for s in listed)) for p, listed in sends.items()}
+        fresh = has_slot[slot] - lookup(me, relayed)
+
+        @pl.when(fresh == 1)
         def _():
-            pltpu.make_async_copy(mf.at[other], mf.at[other], mrecv.at[other]).wait()
-            split_factor(other)
+            for chunk in range(CHUNKS):
+                wait_block(slot, chunk)
+
+    def message(slot):
+        @pl.when((has_slot[slot] == 1) & (other_of[slot] != row))
+        def _():
             def body(t, carry):
                 part_of = pl.ds(pl.multiple_of(t * BLOCK, BLOCK), BLOCK)
-                turned = split(source[:, part_of].T)
+                turned = split(kbuf[slot, :, part_of].T)
                 outm[slot, part_of, :] = dot3(turned, (mhi[row], mlo[row]))
                 return carry
             lax.fori_loop(0, SIDE, body, 0)
@@ -362,16 +374,26 @@
                 def _(place=place, taker=slots[slot][0]):
                     product_copy(place[0], slot, taker).start()
 
-        @pl.when(has == 1)
+    def collect(slot):
+        other = other_of[slot]
+
+        @pl.when((has_slot[slot] == 1) & (other != row))
+        def _():
+            pltpu.make_async_copy(mf.at[other], mf.at[other], mrecv.at[other]).wait()
+            split_factor(other)
+
+        @pl.when(has_slot[slot] == 1)
         def _():
             def body(t, carry):
                 part_of = pl.ds(pl.multiple_of(t * BLOCK, BLOCK), BLOCK)
-                straight = split(source[part_of, :])
+                straight = split(kbuf[slot, part_of, :])
                 acc[part_of, :] += dot3(straight, (mhi[other], mlo[other]))
                 return carry
             lax.fori_loop(0, SIDE, body, 0)
 
-    work(0)
+    message(0)
+    relay(range(0, 3))
+    collect(0)
     for place, listed in sends.items():
         late = [(i, s) for i, s in enumerate(listed) if s[3]]
         if late:
@@ -380,9 +402,17 @@
                 for chunk in range(CHUNKS):
                     for index, (source_slot, target, slot, _) in late:
                         block_copy(index, source_slot, target, slot, chunk).start()
-    relay(range(CHUNKS // 2, CHUNKS))
-    for slot in range(1, SIDE):
-        work(slot)
+    arrive(1)
+    message(1)
+    relay(range(3, 6))
+    collect(1)
+    relay(range(6, CHUNKS))
+    arrive(2)
+    message(2)
+    collect(2)
+    arrive(3)
+    message(3)
+    collect(3)
 
     for sender in range(SIDE):
         gets = lookup(me, {
@@ -484,7 +514,6 @@
     wide = 3 * BLOCK
     f32 = jnp.float32
     most = max(len(listed) for listed in transfers()[1].values())
-    smem = pl.BlockSpec(memory_space=pltpu.SMEM)
     vmem = pl.BlockSpec(memory_space=pltpu.VMEM)
     dma = pltpu.SemaphoreType.DMA
     return pl.pallas_call(
@@ -496,10 +525,17 @@
             jax.ShapeDtypeStruct((1, 3, BLOCK, BLOCK), f32),
             jax.ShapeDtypeStruct((3, 1, BLOCK, BLOCK), f32),
         ),
-        in_specs=[smem] * 3 + [vmem] * 6,
+        in_specs=[pl.BlockSpec(memory_space=pl.ANY)] * 9,
         out_specs=[vmem] * 5,
         scratch_shapes=[
-            pltpu.VMEM((SIDE - 1, rows, rows), f32),
+            pltpu.SMEM(structure.shape, jnp.int32),
+            pltpu.SMEM(pick_second.shape, jnp.int32),
+            pltpu.SMEM(pick_third.shape, jnp.int32),
+            pltpu.VMEM((3, rows, BLOCK), f32),
+            pltpu.VMEM(ancestor.shape, f32),
+            pltpu.VMEM(diag_inverse.shape, f32),
+            dma((9,)),
+            pltpu.VMEM((SIDE, rows, rows), f32),
             pltpu.VMEM((SIDE, rows, wide), f32),
             pltpu.VMEM((SIDE, rows, wide), jnp.bfloat16),
             pltpu.VMEM((SIDE, rows, wide), jnp.bfloat16),
@@ -521,7 +557,7 @@
             dma((3,)),
         ],
         compiler_params=pltpu.CompilerParams(
-            collective_id=0, has_side_effects=True, vmem_limit_bytes=40 * 1024 * 1024
+            collective_id=0, has_side_effects=True, vmem_limit_bytes=60 * 1024 * 1024
         ),
     )(
         structure, pick_second, pick_third, known_inverse, lower_first, lower_second, lower_third,

time: 93.5 us -> 81.3 us (0.87)
  the two profiles are of different devices: /device:TPU:19 before, /device:TPU:0 now
where the time goes in v2:
time: 81.3 us; the launch traced here: 81.1 us
  Pallas kernels  75 us (92%)
  local copies, waits for them, and re-layouts  5.45 us (7%)
    pallas_call x1, Pallas kernels, on_device_fused(): pl.pallas_call(fused_kernel, out_shape=(jax.ShapeDtypeStruct((rows, BLOCK...  75 us
    unnamed x13, local copies, waits for them, and re-layouts  5.45 us

profile of v2, /device:TPU:0, one launch (start us, length us, event | category | flops | bytes accessed | tf_op | source)
XLA Modules:
  0.0 81.1 jit_solution(2980042725934870780)
XLA Ops:
  0.6 75.0 %shard_map.128 = (f32[512,128]{1,0:T(8,128)}, f32[512,128]{1,0:T(8,128)}, f32[512,128]{1,0:T(8,128)}, f32[1,3,128,128]{3,2,1,0:T(8,128)}, f32[3,1,128,128]{3,2,1,0:T(8,128)}) custom-call(s32[4,8]{1,0:T(4,128)} %structure_in.1, s32[4,7]{1,0:T(4,128)} %second_in.1, s32[4,6]{1,0:T(4,128)} %third_in.1, f32[512,512]{1,0:T(8,128)} %k_ref.1, f32[512,128]{1,0:T(8,128)} %l1_in.1, ...), custom_call_target="tpu_custom_call" | custom-call | tf_op jit(solution)/shard_map/pallas_call | solution.py:519
  75.7 0.0 copy-start.1
  75.7 1.7 %copy.19 = f32[512,128]{1,0:T(8,128)} copy(f32[512,128]{1,0:T(8,128)} %get-tuple-element.10) | data formatting | bytes 524288
  77.4 0.0 copy-done.1
  77.4 0.0 copy-start
  77.4 0.7 copy.20
  78.1 0.3 copy-done
  78.4 0.0 copy-start.3
  78.4 0.7 copy.21
  79.1 0.3 copy-done.3
  79.4 0.0 copy-start.2
  79.4 0.7 copy.22
  80.1 0.3 copy-done.2
  80.4 0.7 copy.23
Async XLA Ops:
  75.7 1.7 %copy-start.1 = (f32[512,128]{1,0:T(8,128)S(1)}, f32[512,128]{1,0:T(8,128)}, u32[]{:S(2)}) copy-start(f32[512,128]{1,0:T(8,128)} %get-tuple-element.11) | copy-start | bytes 786436
  77.4 1.0 %copy-start = (f32[512,128]{1,0:T(8,128)S(1)}, f32[512,128]{1,0:T(8,128)}, u32[]{:S(2)}) copy-start(f32[512,128]{1,0:T(8,128)} %get-tuple-element.12) | copy-start | bytes 786436
  78.4 1.0 %copy-start.3 = (f32[1,3,128,128]{3,2,1,0:T(8,128)S(1)}, f32[1,3,128,128]{3,2,1,0:T(8,128)}, u32[]{:S(2)}) copy-start(f32[1,3,128,128]{3,2,1,0:T(8,128)} %get-tuple-element.13) | copy-start | bytes 589828
  79.4 1.0 %copy-start.2 = (f32[3,1,128,128]{3,2,1,0:T(8,128)S(1)}, f32[3,1,128,128]{3,2,1,0:T(8,128)}, u32[]{:S(2)}) copy-start(f32[3,1,128,128]{3,2,1,0:T(8,128)} %get-tuple-element.14) | copy-start | bytes 589828

commit v3 on v2

--- a/solution.py
+++ b/solution.py
@@ -153,7 +153,7 @@
 def landing_plan():
     half = {
         (0, 0): [],
-        (1, 0): [(2, 2, False), (3, 3, True), (1, 1, True)],
+        (1, 0): [(2, 2, False), (3, 2, False), (1, 1, True)],
         (2, 0): [(2, 1, False)],
         (3, 0): [(2, 1, False), (3, 1, False)],
         (0, 1): [(0, 0, False)],
@@ -183,6 +183,36 @@
     return plan, sends
 
 
+FOLDS = {(3, 1): 2, (0, 2): 1}
+
+
+def product_sends(plan):
+    return {
+        (place, slot): entry[0]
+        for place, slots in plan.items()
+        for slot, entry in enumerate(slots)
+        if entry[0] != place[0] and not (place in FOLDS and slot == 1)
+    }
+
+
+def factor_sends(plan):
+    direct = {place: [] for place in plan}
+    passes = {}
+    for owner, col in plan:
+        takers = [
+            row for row in range(SIDE)
+            if row != owner and any(entry[0] == owner for entry in plan[row, col])
+        ]
+        near = (owner + 2) % SIDE
+        far = near + 1 - 2 * (near % 2)
+        if near in takers and far in takers:
+            takers.remove(far)
+            assert (near, col) not in passes
+            passes[near, col] = (owner, far)
+        direct[owner, col] = takers
+    return direct, passes
+
+
 def lookup(me, values):
     total = jnp.int32(0)
     for place, value in values.items():
@@ -209,8 +239,8 @@
     structure_in, second_in, third_in, k_ref, l1_in, l2_in, l3_in, anc_in, dinv_in,
     first_ref, second_out, third_out, ancestral_ref, diagonal_ref,
     structure_ref, second_ref, third_ref, lbuf, anc_ref, dinv_ref, copied,
-    kbuf, mf, mhi, mlo, acc, outm, pin, part, got_core, half_sum, got_row, total,
-    ksend, krecv, msend, mrecv, psend, precv, rsend, rrecv,
+    kbuf, mf, mhi, mlo, acc, outm, pin, fold, part, got_core, half_sum, got_row, total,
+    ksend, krecv, msend, mrecv, psend, precv, fsem, rsend, rrecv,
 ):
     row = lax.axis_index("row")
     col = lax.axis_index("col")
@@ -238,6 +268,19 @@
         rows = pl.ds(chunk * step_rows, step_rows)
         pltpu.make_async_copy(k_ref.at[rows], kbuf.at[slot, rows], krecv.at[slot - 1, chunk]).wait()
 
+    def fold_copy(taker):
+        return pltpu.make_async_remote_copy(
+            src_ref=outm.at[1],
+            dst_ref=fold,
+            send_sem=psend.at[1],
+            recv_sem=fsem,
+            device_id={"row": taker},
+            device_id_type=MESH,
+        )
+
+    def wait_factor(owner):
+        pltpu.make_async_copy(mf.at[owner], mf.at[owner], mrecv.at[owner]).wait()
+
     def factor_copy(owner, taker):
         return pltpu.make_async_remote_copy(
             src_ref=mf.at[owner],
@@ -305,17 +348,14 @@
             columns = slice(level * BLOCK, (level + 1) * BLOCK)
             mf[row, rows, columns] = lbuf[level, rows, :] * keep[level][i]
 
-    needs = {place: [] for place in plan}
-    for (r, k), slots in plan.items():
-        for slot, (other, _, _) in enumerate(slots):
-            if other != r:
-                needs[other, k].append((slot, r))
-    for (b, k), takers in needs.items():
+    direct, passes = factor_sends(plan)
+    products = product_sends(plan)
+    for place, takers in direct.items():
         if takers:
-            @at((b, k))
-            def _(b=b, takers=takers):
-                for _, taker in sorted(takers):
-                    factor_copy(b, taker).start()
+            @at(place)
+            def _(place=place, takers=takers):
+                for taker in takers:
+                    factor_copy(place[0], taker).start()
 
     acc[...] = jnp.zeros_like(acc)
 
@@ -330,9 +370,9 @@
 
     split_factor(row)
 
-    def relay(chunks):
+    def relay(chunks, slots_passed):
         for place, listed in sends.items():
-            passed = [(i, s) for i, s in enumerate(listed) if s[0] != 0]
+            passed = [(i, s) for i, s in enumerate(listed) if s[0] in slots_passed]
             if passed:
                 @at(place)
                 def _(passed=passed):
@@ -368,18 +408,37 @@
                 return carry
             lax.fori_loop(0, SIDE, body, 0)
 
-        for place, slots in plan.items():
-            if len(slots) > slot and slots[slot][0] != place[0]:
+        if slot == 1:
+            for place, taker in FOLDS.items():
                 @at(place)
-                def _(place=place, taker=slots[slot][0]):
+                def _(taker=taker):
+                    fold_copy(taker).start()
+
+                @at((taker, place[1]))
+                def _():
+                    pltpu.make_async_copy(outm.at[1], fold, fsem).wait()
+                    outm[1] += fold[...]
+
+        for (place, at_slot), taker in products.items():
+            if at_slot == slot:
+                @at(place)
+                def _(place=place, taker=taker):
                     product_copy(place[0], slot, taker).start()
 
     def collect(slot):
         other = other_of[slot]
 
+        passed = lookup(me, {
+            p: 1 for p, (owner, _) in passes.items()
+            if len(plan[p]) > slot and plan[p][slot][0] == owner
+        })
+
+        @pl.when((has_slot[slot] == 1) & (other != row) & (passed == 0))
+        def _():
+            wait_factor(other)
+
         @pl.when((has_slot[slot] == 1) & (other != row))
         def _():
-            pltpu.make_async_copy(mf.at[other], mf.at[other], mrecv.at[other]).wait()
             split_factor(other)
 
         @pl.when(has_slot[slot] == 1)
@@ -391,9 +450,48 @@
                 return carry
             lax.fori_loop(0, SIDE, body, 0)
 
+    every = range(1, SIDE)
     message(0)
-    relay(range(0, 3))
+    relay(range(0, 3), every)
+    for place, (owner, taker) in passes.items():
+        @at(place)
+        def _(owner=owner, taker=taker, place=place):
+            wait_factor(owner)
+            pltpu.make_async_remote_copy(
+                src_ref=mf.at[owner],
+                dst_ref=mf.at[owner],
+                send_sem=msend.at[place[0]],
+                recv_sem=mrecv.at[owner],
+                device_id={"row": taker},
+                device_id_type=MESH,
+            ).start()
+    relay(range(3, 4), every)
     collect(0)
+    relay(range(4, 6), every)
+    relay(range(6, CHUNKS), [1])
+    arrive(1)
+    message(1)
+    relay(range(6, 7), [2, 3])
+    collect(1)
+    relay(range(7, CHUNKS), [2, 3])
+    arrive(2)
+    message(2)
+    collect(2)
+    arrive(3)
+    message(3)
+    collect(3)
+
+    for sender in range(SIDE):
+        gets = lookup(me, {
+            p: 1 for p in plan
+            if any(q == (sender, p[1]) and taker == p[0] for (q, _), taker in products.items())
+        })
+
+        @pl.when(gets == 1)
+        def _(sender=sender):
+            pltpu.make_async_copy(outm.at[0], pin.at[sender], precv.at[sender]).wait()
+            acc[...] += pin[sender]
+
     for place, listed in sends.items():
         late = [(i, s) for i, s in enumerate(listed) if s[3]]
         if late:
@@ -402,28 +500,6 @@
                 for chunk in range(CHUNKS):
                     for index, (source_slot, target, slot, _) in late:
                         block_copy(index, source_slot, target, slot, chunk).start()
-    arrive(1)
-    message(1)
-    relay(range(3, 6))
-    collect(1)
-    relay(range(6, CHUNKS))
-    arrive(2)
-    message(2)
-    collect(2)
-    arrive(3)
-    message(3)
-    collect(3)
-
-    for sender in range(SIDE):
-        gets = lookup(me, {
-            p: 1 for p in plan
-            if p[0] != sender and any(s[0] == p[0] for s in plan[sender, p[1]])
-        })
-
-        @pl.when(gets == 1)
-        def _(sender=sender):
-            pltpu.make_async_copy(outm.at[0], pin.at[sender], precv.at[sender]).wait()
-            acc[...] += pin[sender]
 
     def kept(value, level):
         return jnp.concatenate(
@@ -499,11 +575,15 @@
             for index, (source_slot, target, slot, _) in enumerate(listed):
                 for chunk in range(CHUNKS):
                     block_copy(index, source_slot, target, slot, chunk).wait_send()
-            for _, taker in needs[place]:
+            for taker in direct[place]:
                 factor_copy(place[0], taker).wait_send()
-            for slot, (other, _, _) in enumerate(plan[place]):
-                if other != place[0]:
-                    product_copy(place[0], slot, other).wait_send()
+            if place in passes:
+                pltpu.make_async_copy(mf.at[0], mf.at[0], msend.at[place[0]]).wait()
+            if place in FOLDS:
+                fold_copy(FOLDS[place]).wait_send()
+            for (origin, slot), taker in products.items():
+                if origin == place:
+                    product_copy(place[0], slot, taker).wait_send()
 
 
 def on_device_fused(
@@ -542,6 +622,7 @@
             pltpu.VMEM((rows, wide), f32),
             pltpu.VMEM((SIDE, rows, wide), f32),
             pltpu.VMEM((SIDE, rows, wide), f32),
+            pltpu.VMEM((rows, wide), f32),
             pltpu.VMEM((2, 3, BLOCK, BLOCK), f32),
             pltpu.VMEM((3, BLOCK, BLOCK), f32),
             pltpu.VMEM((3, BLOCK, BLOCK), f32),
@@ -553,6 +634,7 @@
             dma((SIDE,)),
             dma((SIDE,)),
             dma((SIDE,)),
+            dma,
             dma((3,)),
             dma((3,)),
         ],

time: 81.3 us -> 73.4 us (0.903)
  Pallas kernels: 75 us -> 67.1 us
    pallas_call x1, Pallas kernels: 75 us -> 67.1 us  [on_device_fused(): pl.pallas_call(fused_kernel, out_shape=(jax.ShapeDtypeStruct((rows, BLOCK...]
where the time goes in v3:
time: 73.4 us; the launch traced here: 73.2 us
  Pallas kernels  67.1 us (91%)
  local copies, waits for them, and re-layouts  5.45 us (7%)
    pallas_call x1, Pallas kernels, on_device_fused(): pl.pallas_call(fused_kernel, out_shape=(jax.ShapeDtypeStruct((rows, BLOCK...  67.1 us
    unnamed x13, local copies, waits for them, and re-layouts  5.45 us

profile of v3, /device:TPU:0, one launch (start us, length us, event | category | flops | bytes accessed | tf_op | source)
XLA Modules:
  0.0 73.2 jit_solution(2489043926971204068)
XLA Ops:
  0.6 67.1 %shard_map.128 = (f32[512,128]{1,0:T(8,128)}, f32[512,128]{1,0:T(8,128)}, f32[512,128]{1,0:T(8,128)}, f32[1,3,128,128]{3,2,1,0:T(8,128)}, f32[3,1,128,128]{3,2,1,0:T(8,128)}) custom-call(s32[4,8]{1,0:T(4,128)} %structure_in.1, s32[4,7]{1,0:T(4,128)} %second_in.1, s32[4,6]{1,0:T(4,128)} %third_in.1, f32[512,512]{1,0:T(8,128)} %k_ref.1, f32[512,128]{1,0:T(8,128)} %l1_in.1, ...), custom_call_target="tpu_custom_call" | custom-call | tf_op jit(solution)/shard_map/pallas_call | solution.py:599
  67.7 0.0 copy-start.1
  67.7 1.7 %copy.19 = f32[512,128]{1,0:T(8,128)} copy(f32[512,128]{1,0:T(8,128)} %get-tuple-element.10) | data formatting | bytes 524288
  69.5 0.0 copy-done.1
  69.5 0.0 copy-start
  69.5 0.7 copy.20
  70.2 0.3 copy-done
  70.5 0.0 copy-start.3
  70.5 0.7 copy.21
  71.2 0.3 copy-done.3
  71.5 0.0 copy-start.2
  71.5 0.7 copy.22
  72.2 0.3 copy-done.2
  72.5 0.7 copy.23
Async XLA Ops:
  67.7 1.7 %copy-start.1 = (f32[512,128]{1,0:T(8,128)S(1)}, f32[512,128]{1,0:T(8,128)}, u32[]{:S(2)}) copy-start(f32[512,128]{1,0:T(8,128)} %get-tuple-element.11) | copy-start | bytes 786436
  69.5 1.0 %copy-start = (f32[512,128]{1,0:T(8,128)S(1)}, f32[512,128]{1,0:T(8,128)}, u32[]{:S(2)}) copy-start(f32[512,128]{1,0:T(8,128)} %get-tuple-element.12) | copy-start | bytes 786436
  70.5 1.0 %copy-start.3 = (f32[1,3,128,128]{3,2,1,0:T(8,128)S(1)}, f32[1,3,128,128]{3,2,1,0:T(8,128)}, u32[]{:S(2)}) copy-start(f32[1,3,128,128]{3,2,1,0:T(8,128)} %get-tuple-element.13) | copy-start | bytes 589828
  71.5 1.0 %copy-start.2 = (f32[3,1,128,128]{3,2,1,0:T(8,128)S(1)}, f32[3,1,128,128]{3,2,1,0:T(8,128)}, u32[]{:S(2)}) copy-start(f32[3,1,128,128]{3,2,1,0:T(8,128)} %get-tuple-element.14) | copy-start | bytes 589828

commit v4 on v3

--- a/solution.py
+++ b/solution.py
@@ -153,18 +153,18 @@
 def landing_plan():
     half = {
         (0, 0): [],
-        (1, 0): [(2, 2, False), (3, 2, False), (1, 1, True)],
-        (2, 0): [(2, 1, False)],
-        (3, 0): [(2, 1, False), (3, 1, False)],
-        (0, 1): [(0, 0, False)],
+        (1, 0): [(2, 2, 0), (3, 2, 0), (1, 1, 2)],
+        (2, 0): [(2, 1, 0)],
+        (3, 0): [(2, 1, 0), (3, 1, 0)],
+        (0, 1): [(0, 0, 0)],
         (1, 1): [],
-        (2, 1): [(0, 0, False), (2, 2, False)],
-        (3, 1): [(0, 0, False), (2, 2, False), (3, 3, False)],
+        (2, 1): [(0, 0, 0), (2, 2, 0)],
+        (3, 1): [(0, 0, 1), (2, 2, 0), (3, 3, 0)],
     }
     plan = {}
     for (row, col), slots in half.items():
-        plan[row, col] = [(col, None, False)] + slots
-        plan[3 - row, 3 - col] = [(3 - col, None, False)] + [
+        plan[row, col] = [(col, None, 0)] + slots
+        plan[3 - row, 3 - col] = [(3 - col, None, 0)] + [
             (3 - other, 3 - source, late) for other, source, late in slots
         ]
     return plan
@@ -252,21 +252,29 @@
     def at(place):
         return pl.when(me == place[0] * SIDE + place[1])
 
+    def piece(chunk, diagonal):
+        half = rows_of // 2
+        low = diagonal and chunk * step_rows >= half
+        columns = pl.ds(half, half) if low else pl.ds(0, rows_of)
+        return pl.ds(chunk * step_rows, step_rows), columns
+
     def block_copy(index, source_slot, target, slot, chunk):
-        rows = pl.ds(chunk * step_rows, step_rows)
-        source = k_ref.at[rows] if source_slot == 0 else kbuf.at[source_slot, rows]
+        area = piece(chunk, plan[target][slot][0] == target[0])
+        source = k_ref.at[area] if source_slot == 0 else kbuf.at[(source_slot, *area)]
         return pltpu.make_async_remote_copy(
             src_ref=source,
-            dst_ref=kbuf.at[slot, rows],
+            dst_ref=kbuf.at[(slot, *area)],
             send_sem=ksend.at[index, chunk],
             recv_sem=krecv.at[slot - 1, chunk],
             device_id={"col": target[1]},
             device_id_type=MESH,
         )
 
-    def wait_block(slot, chunk):
-        rows = pl.ds(chunk * step_rows, step_rows)
-        pltpu.make_async_copy(k_ref.at[rows], kbuf.at[slot, rows], krecv.at[slot - 1, chunk]).wait()
+    def wait_block(slot, chunk, diagonal):
+        area = piece(chunk, diagonal)
+        pltpu.make_async_copy(
+            k_ref.at[area], kbuf.at[(slot, *area)], krecv.at[slot - 1, chunk]
+        ).wait()
 
     def fold_copy(taker):
         return pltpu.make_async_remote_copy(
@@ -375,10 +383,10 @@
             passed = [(i, s) for i, s in enumerate(listed) if s[0] in slots_passed]
             if passed:
                 @at(place)
-                def _(passed=passed):
+                def _(passed=passed, place=place):
                     for chunk in chunks:
                         for index, (source_slot, target, slot, _) in passed:
-                            wait_block(source_slot, chunk)
+                            wait_block(source_slot, chunk, plan[place][source_slot][0] == place[0])
                             block_copy(index, source_slot, target, slot, chunk).start()
 
     for copy in local[6:]:
@@ -393,10 +401,15 @@
         relayed = {p: int(any(s[0] == slot for s in listed)) for p, listed in sends.items()}
         fresh = has_slot[slot] - lookup(me, relayed)
 
-        @pl.when(fresh == 1)
+        @pl.when((fresh == 1) & (other_of[slot] != row))
         def _():
             for chunk in range(CHUNKS):
-                wait_block(slot, chunk)
+                wait_block(slot, chunk, False)
+
+        @pl.when((fresh == 1) & (other_of[slot] == row))
+        def _():
+            for chunk in range(CHUNKS):
+                wait_block(slot, chunk, True)
 
     def message(slot):
         @pl.when((has_slot[slot] == 1) & (other_of[slot] != row))
@@ -441,6 +454,12 @@
         def _():
             split_factor(other)
 
+        if slot > 0:
+            @pl.when((has_slot[slot] == 1) & (other == row))
+            def _():
+                half = rows_of // 2
+                kbuf[slot, half:, :half] = kbuf[slot, :half, half:].T
+
         @pl.when(has_slot[slot] == 1)
         def _():
             def body(t, carry):
@@ -449,6 +468,16 @@
                 acc[part_of, :] += dot3(straight, (mhi[other], mlo[other]))
                 return carry
             lax.fori_loop(0, SIDE, body, 0)
+
+    def start_late(stage):
+        for place, listed in sends.items():
+            late = [(i, s) for i, s in enumerate(listed) if s[3] == stage]
+            if late:
+                @at(place)
+                def _(late=late):
+                    for chunk in range(CHUNKS):
+                        for index, (source_slot, target, slot, _) in late:
+                            block_copy(index, source_slot, target, slot, chunk).start()
 
     every = range(1, SIDE)
     message(0)
@@ -467,6 +496,7 @@
             ).start()
     relay(range(3, 4), every)
     collect(0)
+    start_late(1)
     relay(range(4, 6), every)
     relay(range(6, CHUNKS), [1])
     arrive(1)
@@ -492,14 +522,7 @@
             pltpu.make_async_copy(outm.at[0], pin.at[sender], precv.at[sender]).wait()
             acc[...] += pin[sender]
 
-    for place, listed in sends.items():
-        late = [(i, s) for i, s in enumerate(listed) if s[3]]
-        if late:
-            @at(place)
-            def _(late=late):
-                for chunk in range(CHUNKS):
-                    for index, (source_slot, target, slot, _) in late:
-                        block_copy(index, source_slot, target, slot, chunk).start()
+    start_late(2)
 
     def kept(value, level):
         return jnp.concatenate(
@@ -586,6 +609,15 @@
                     product_copy(place[0], slot, taker).wait_send()
 
 
+def store_kernel(*refs):
+    sems = refs[10]
+    copies = [pltpu.make_async_copy(refs[i], refs[i + 5], sems.at[i]) for i in range(5)]
+    for copy in copies:
+        copy.start()
+    for copy in copies:
+        copy.wait()
+
+
 def on_device_fused(
     known_inverse, lower_first, lower_second, lower_third, ancestor, diag_inverse,
     structure, pick_second, pick_third,
@@ -596,7 +628,7 @@
     most = max(len(listed) for listed in transfers()[1].values())
     vmem = pl.BlockSpec(memory_space=pltpu.VMEM)
     dma = pltpu.SemaphoreType.DMA
-    return pl.pallas_call(
+    results = pl.pallas_call(
         fused_kernel,
         out_shape=(
             jax.ShapeDtypeStruct((rows, BLOCK), f32),
@@ -645,6 +677,15 @@
         structure, pick_second, pick_third, known_inverse, lower_first, lower_second, lower_third,
         ancestor, diag_inverse,
     )
+    anywhere = pl.BlockSpec(memory_space=pl.ANY)
+    return pl.pallas_call(
+        store_kernel,
+        out_shape=tuple(jax.ShapeDtypeStruct(one.shape, one.dtype) for one in results),
+        in_specs=[anywhere] * 5,
+        out_specs=[anywhere] * 5,
+        scratch_shapes=[dma((5,))],
+        compiler_params=pltpu.CompilerParams(vmem_limit_bytes=60 * 1024 * 1024),
+    )(*results)
 
 
 def solution(mesh):

time: 73.4 us -> 99 us (1.35)
  Pallas kernels: 67.1 us -> 97.8 us
  local copies, waits for them, and re-layouts: 5.45 us -> 0 us
    pallas_call x0 -> x1, Pallas kernels: none -> 36.9 us  [on_device_fused(): pl.pallas_call(store_kernel, out_shape=tuple((jax.ShapeDtypeStruct(one.sh...]
    pallas_call x1, Pallas kernels: 67.1 us -> 60.9 us  [on_device_fused(): pl.pallas_call(fused_kernel, out_shape=(jax.ShapeDtypeStruct((rows, BLOCK...]
    unnamed x13 -> x0, local copies, waits for them, and re-layouts: 5.45 us -> none
where the time goes in v4:
time: 99 us; the launch traced here: 98.4 us
  Pallas kernels  97.8 us (99%)
    pallas_call x1, Pallas kernels, on_device_fused(): pl.pallas_call(fused_kernel, out_shape=(jax.ShapeDtypeStruct((rows, BLOCK...  60.9 us
    pallas_call x1, Pallas kernels, on_device_fused(): pl.pallas_call(store_kernel, out_shape=tuple((jax.ShapeDtypeStruct(one.sh...  36.9 us

profile of v4, /device:TPU:0, one launch (start us, length us, event | category | flops | bytes accessed | tf_op | source)
XLA Modules:
  0.0 98.4 jit_solution(7490325153339026550)
XLA Ops:
  0.6 60.9 %shard_map.128 = (f32[512,128]{1,0:T(8,128)}, f32[512,128]{1,0:T(8,128)}, f32[512,128]{1,0:T(8,128)}, f32[1,3,128,128]{3,2,1,0:T(8,128)}, f32[3,1,128,128]{3,2,1,0:T(8,128)}) custom-call(s32[4,8]{1,0:T(4,128)} %structure_in.1, s32[4,7]{1,0:T(4,128)} %second_in.1, s32[4,6]{1,0:T(4,128)} %third_in.1, f32[512,512]{1,0:T(8,128)} %k_ref.1, f32[512,128]{1,0:T(8,128)} %l1_in.1, ...), custom_call_target="tpu_custom_call" | custom-call | tf_op jit(solution)/shard_map/pallas_call | solution.py:631
  61.5 36.9 %shard_map.129 = (f32[512,128]{1,0:T(8,128)}, f32[512,128]{1,0:T(8,128)}, f32[512,128]{1,0:T(8,128)}, f32[1,3,128,128]{3,2,1,0:T(8,128)}, f32[3,1,128,128]{3,2,1,0:T(8,128)}) custom-call(f32[512,128]{1,0:T(8,128)} %get-tuple-element.10.refs_0_, f32[512,128]{1,0:T(8,128)} %get-tuple-element.11.refs_1_, f32[512,128]{1,0:T(8,128)} %get-tuple-element.12.refs_2_, ...), custom_call_target="tpu_custom_call" | custom-call | tf_op jit(solution)/shard_map/pallas_call | solution.py:681

commit v5 on v4

--- a/solution.py
+++ b/solution.py
@@ -610,11 +610,15 @@
 
 
 def store_kernel(*refs):
-    sems = refs[10]
-    copies = [pltpu.make_async_copy(refs[i], refs[i + 5], sems.at[i]) for i in range(5)]
-    for copy in copies:
+    held, sems = refs[10:15], refs[15]
+    loads = [pltpu.make_async_copy(refs[i], held[i], sems.at[i]) for i in range(5)]
+    stores = [pltpu.make_async_copy(held[i], refs[i + 5], sems.at[i + 5]) for i in range(5)]
+    for copy in loads:
         copy.start()
-    for copy in copies:
+    for load, store in zip(loads, stores):
+        load.wait()
+        store.start()
+    for copy in stores:
         copy.wait()
 
 
@@ -683,7 +687,7 @@
         out_shape=tuple(jax.ShapeDtypeStruct(one.shape, one.dtype) for one in results),
         in_specs=[anywhere] * 5,
         out_specs=[anywhere] * 5,
-        scratch_shapes=[dma((5,))],
+        scratch_shapes=[pltpu.VMEM(one.shape, f32) for one in results] + [dma((10,))],
         compiler_params=pltpu.CompilerParams(vmem_limit_bytes=60 * 1024 * 1024),
     )(*results)
 

time: 99 us -> 64.1 us (0.65)
  Pallas kernels: 97.8 us -> 62.9 us
    pallas_call x1, Pallas kernels: 36.9 us -> 2.04 us  [on_device_fused(): pl.pallas_call(store_kernel, out_shape=tuple((jax.ShapeDtypeStruct(one.sh...]
where the time goes in v5:
time: 64.1 us; the launch traced here: 63.6 us
  Pallas kernels  62.9 us (98%)
    pallas_call x1, Pallas kernels, on_device_fused(): pl.pallas_call(fused_kernel, out_shape=(jax.ShapeDtypeStruct((rows, BLOCK...  60.9 us
    pallas_call x1, Pallas kernels, on_device_fused(): pl.pallas_call(store_kernel, out_shape=tuple((jax.ShapeDtypeStruct(one.sh...  2.04 us

profile of v5, /device:TPU:0, one launch (start us, length us, event | category | flops | bytes accessed | tf_op | source)
XLA Modules:
  0.0 63.6 jit_solution(9127953707770726320)
XLA Ops:
  0.6 60.9 %shard_map.128 = (f32[512,128]{1,0:T(8,128)}, f32[512,128]{1,0:T(8,128)}, f32[512,128]{1,0:T(8,128)}, f32[1,3,128,128]{3,2,1,0:T(8,128)}, f32[3,1,128,128]{3,2,1,0:T(8,128)}) custom-call(s32[4,8]{1,0:T(4,128)} %structure_in.1, s32[4,7]{1,0:T(4,128)} %second_in.1, s32[4,6]{1,0:T(4,128)} %third_in.1, f32[512,512]{1,0:T(8,128)} %k_ref.1, f32[512,128]{1,0:T(8,128)} %l1_in.1, ...), custom_call_target="tpu_custom_call" | custom-call | tf_op jit(solution)/shard_map/pallas_call | solution.py:635
  61.5 2.0 %shard_map.129 = (f32[512,128]{1,0:T(8,128)}, f32[512,128]{1,0:T(8,128)}, f32[512,128]{1,0:T(8,128)}, f32[1,3,128,128]{3,2,1,0:T(8,128)}, f32[3,1,128,128]{3,2,1,0:T(8,128)}) custom-call(f32[512,128]{1,0:T(8,128)} %get-tuple-element.10.refs_0_, f32[512,128]{1,0:T(8,128)} %get-tuple-element.11.refs_1_, f32[512,128]{1,0:T(8,128)} %get-tuple-element.12.refs_2_, ...), custom_call_target="tpu_custom_call" | custom-call | tf_op jit(solution)/shard_map/pallas_call | solution.py:685
